TPU v7x, 512 devices: a whole 4x4x16 slice. The times are simulated.
512 devices in a mesh: section: 8 (over z_lo), seq: 64 (over z_hi, x, y, core).
Axes of the slice: x: 4, y: 4, z: 16 (z_hi: 2, z_lo: 8; z = z_hi * 8 + z_lo), core: 2. Of those that a mesh axis runs over, the one named last changes fastest.
Arguments:
- queries: bfloat16 [24576, 4096], P('seq', 'section'), may hold values from -8 to 8
- enc_keys: bfloat16 [512, 4096], P(('section', 'seq')), may hold values from -8 to 8
- enc_values: bfloat16 [512, 4096], P(('section', 'seq')), may hold values from -6 to 6
- out_grad: bfloat16 [24576, 4096], P('seq', 'section'), may hold values from -6 to 6
- enc_doc: int32 [512], replicated, may hold values from 0 to 3, never falling along the last dimension, each value on 1 to 256 neighbouring positions
- dec_doc: int32 [24576], P('seq'), may hold values from 0 to 3, never falling along the last dimension, each value on 1 to 12288 neighbouring positions
Outputs:
- context: bfloat16 [24576, 4096], P('seq', 'section')
- query_grad: float32 [24576, 4096], P('seq', 'section')
- key_grad: float32 [512, 4096], P(('section', 'seq'))
- value_grad: float32 [512, 4096], P(('section', 'seq'))
Inputs may be any that keep to these rules, and one draw needn't show every extreme that they name: `enc_doc`: never falls along the positions; every document number occurs. `dec_doc`: never falls along the positions; every document number occurs.
All inputs are finite; a program needn't handle non-finite values.
Results may differ from a plain program's by a relative error of at most 0.02.
The roundings to bfloat16 on the way count: a program that leaves them out, or rounds other values in their place, can miss the bound.
Values may be sent and summed in bfloat16 or wider, within the bound.
No kernel may reach another device: no remote copies, remote signals or barrier semaphores. Data moves between devices by JAX's collectives and lax.ppermute only.
A program may use at most 64 MiB of HBM per device.

v0:
```python
import jax
import jax.numpy as jnp
from jax import lax
from jax.sharding import PartitionSpec as P

HD = 256


NEGATIVE = -1e30


def split_heads(matrix, head_count):
    return matrix.reshape(matrix.shape[0], head_count, matrix.shape[1] // head_count)


def scores_for(q_heads, k_block, doc_rows, doc_block, head_count):
    logits = jnp.einsum(
        "qhd,khd->hqk",
        q_heads,
        split_heads(k_block, head_count),
        preferred_element_type=jnp.float32,
    ) * HD ** (-0.5)
    allowed = (doc_rows[:, None] == doc_block[None, :])[None]
    return (jnp.where(allowed, logits, NEGATIVE), allowed)


def backward_block(
    q_heads, g_heads, doc_rows, log_total, row_delta, key_block, value_block, doc_block, head_count
):
    logits, allowed = scores_for(q_heads, key_block, doc_rows, doc_block, head_count)
    probability = jnp.where(allowed, jnp.exp(logits - log_total[:, :, None]), 0.0)
    prob_grad = jnp.einsum(
        "qhd,khd->hqk",
        g_heads,
        split_heads(value_block, head_count),
        preferred_element_type=jnp.float32,
    )
    dscore = (probability * (prob_grad - row_delta[:, :, None])).astype(jnp.bfloat16)
    row_count = key_block.shape[0]
    key_term = jnp.einsum(
        "hqk,qhd->khd", dscore, q_heads, preferred_element_type=jnp.float32
    ) * HD ** (-0.5)
    value_term = jnp.einsum(
        "hqk,qhd->khd",
        probability.astype(jnp.bfloat16),
        g_heads,
        preferred_element_type=jnp.float32,
    )
    return (
        dscore,
        jnp.concatenate(
            [key_term.reshape(row_count, -1), value_term.reshape(row_count, -1)], axis=1
        ),
    )


def body(queries, enc_keys, enc_values, out_grad, enc_doc, dec_doc):
    sections = lax.axis_size("section")
    shards = lax.axis_size("seq")
    columns = queries.shape[1]
    head_count = columns // HD
    owner_rows = enc_keys.shape[0]
    query_rows = queries.shape[0]
    score_scale = HD ** (-0.5)
    key_part, value_part = (
        lax.all_to_all(enc_keys, "section", split_axis=1, concat_axis=0, tiled=True),
        lax.all_to_all(enc_values, "section", split_axis=1, concat_axis=0, tiled=True),
    )
    doc_keys = enc_doc.reshape(sections, shards, owner_rows).transpose(1, 0, 2).reshape(-1)
    q_heads = split_heads(queries, head_count)
    g_heads = split_heads(out_grad, head_count)
    running = jnp.full((head_count, query_rows), NEGATIVE, jnp.float32)
    key_block = (lax.all_gather(key_part, "seq", axis=0, tiled=True),)[0]
    doc_block = doc_keys
    logits, allowed = scores_for(q_heads, key_block, dec_doc, doc_block, head_count)
    newmax = jnp.maximum(running, jnp.max(logits, axis=2))
    terms = jnp.where(allowed, jnp.exp(logits - newmax[:, :, None]), 0.0)
    normalizer = jnp.sum(terms, axis=2)
    running, normalizer = (newmax, normalizer)
    key_all, value_all = (
        lax.all_gather(key_part, "seq", axis=0, tiled=True),
        lax.all_gather(value_part, "seq", axis=0, tiled=True),
    )
    log_total = running + jnp.log(normalizer)
    total_keys = key_all.shape[0]
    block_size = 512
    number = total_keys // block_size
    blocks = (
        key_all.reshape(number, block_size, columns),
        value_all.reshape(number, block_size, columns),
        doc_keys.reshape(number, block_size),
    )

    def context_step(accumulated, block_item):
        key_block, value_block, doc_block = block_item
        logits, allowed = scores_for(q_heads, key_block, dec_doc, doc_block, head_count)
        weights = jnp.where(allowed, jnp.exp(logits - log_total[:, :, None]), 0.0).astype(
            jnp.bfloat16
        )
        update = jnp.einsum(
            "hqk,khd->qhd",
            weights,
            split_heads(value_block, head_count),
            preferred_element_type=jnp.float32,
        )
        return (accumulated + update, None)

    accumulated, unused = lax.scan(
        context_step, jnp.zeros((query_rows, head_count, HD), jnp.float32), blocks
    )
    context = accumulated.astype(jnp.bfloat16)
    row_delta = jnp.einsum("qhd,qhd->hq", g_heads, context, preferred_element_type=jnp.float32)
    dq_start = jnp.zeros((query_rows, head_count, HD), jnp.float32)

    def walk_keys(dq_sum, block_item):
        key_block, value_block, doc_block = block_item
        dscore, terms = backward_block(
            q_heads,
            g_heads,
            dec_doc,
            log_total,
            row_delta,
            key_block,
            value_block,
            doc_block,
            head_count,
        )
        dq_sum = dq_sum + jnp.einsum(
            "hqk,khd->qhd",
            dscore,
            split_heads(key_block, head_count),
            preferred_element_type=jnp.float32,
        )
        return (dq_sum, terms)

    dq_sum, terms = lax.scan(walk_keys, dq_start, blocks)
    owned_sum = lax.psum_scatter(
        terms.reshape(total_keys, 2 * columns), "seq", scatter_dimension=0, tiled=True
    )
    key_owned = owned_sum[:, :columns]
    value_owned = owned_sum[:, columns:]
    key_grad, value_grad = (
        lax.all_to_all(
            key_owned.astype(jnp.bfloat16), "section", split_axis=0, concat_axis=1, tiled=True
        ).astype(key_owned.dtype),
        lax.all_to_all(
            value_owned.astype(jnp.bfloat16), "section", split_axis=0, concat_axis=1, tiled=True
        ).astype(value_owned.dtype),
    )
    query_grad = (dq_sum * score_scale).reshape(query_rows, columns)
    return (context.reshape(query_rows, columns), query_grad, key_grad, value_grad)


def solution(mesh):
    placed = (
        P("seq", "section"),
        P(("section", "seq"), None),
        P(("section", "seq"), None),
        P("seq", "section"),
        P(),
        P("seq"),
    )
    return jax.shard_map(
        body,
        mesh=mesh,
        in_specs=placed,
        out_specs=(
            P("seq", "section"),
            P("seq", "section"),
            P(("section", "seq"), None),
            P(("section", "seq"), None),
        ),
        check_vma=False,
    )
```

profile of v0, /device:TPU:32, one launch (start us, length us, event | category | flops | bytes accessed | tf_op | source)
XLA Modules:
  0.0 967.3 jit_solution(11728522922914631973)
XLA Ops:
  7.7 1.4 reduce.2
  9.7 12.6 %all-to-all-start.1 = ((bf16[8,2,256]{2,1,0:T(2,128)(2,1)}), bf16[8,2,256]{2,1,0:T(2,128)(2,1)S(1)}, u32[]{:S(2)}, u32[]{:S(2)}) async-start(bf16[8,2,256]{2,1,0:T(2,128)(2,1)} %reshape.178), calls=%async_computation.1 | async-start | bytes 16384 | tf_op jit(solution)/shard_map/all_to_all | solution.py:67
  23.1 1.4 reduce.3
  25.2 6.0 all-to-all-done.1
  31.3 4.7 all-to-all-start
  36.9 1.2 reshape.163
  38.0 1.3 copy.72
  39.6 5.4 all-to-all-done
  45.0 158.4 %all-gather = bf16[1,512,512]{2,1,0:T(8,128)(2,1)S(1)} all-gather(bf16[1,8,512]{2,1,0:T(8,128)(2,1)S(1)} %copy.63), channel_id=2, replica_groups=mesh['section'=8,'seq'=64] {'seq'}, dimensions={1}, use_global_device_ids=true | all-gather | bytes 532480 | tf_op jit(solution)/shard_map/all_gather | solution.py:81
  203.6 147.6 %all-gather.1 = bf16[1,512,512]{2,1,0:T(8,128)(2,1)S(1)} all-gather(bf16[1,8,512]{2,1,0:T(8,128)(2,1)S(1)} %copy.67), channel_id=3, replica_groups=mesh['section'=8,'seq'=64] {'seq'}, dimensions={1}, use_global_device_ids=true | all-gather | bytes 532480 | tf_op jit(solution)/shard_map/all_gather | solution.py:82
  351.2 1.0 copy.68
  353.9 1.3 convolution_convert_fusion
  355.2 1.4 copy.84
  356.6 1.2 multiply_reduce_fusion
  357.8 1.0 copy.85
  358.9 1.8 fusion.1
  362.3 1.9 copy.86
  364.2 566.0 %reduce-scatter.4.cloned.1.call-done = f32[8,1024]{1,0:T(8,128)} async-done(((f32[512,1024]{1,0:T(8,128)}), f32[8,1024]{1,0:T(8,128)}) %reduce-scatter.4.cloned.1.call-update) | async-done | bytes 32784
  932.6 4.5 all-to-all-start.3
  938.4 7.6 all-to-all-done.3
  946.1 4.7 all-to-all-start.2
  951.2 0.9 copy.75
  952.2 1.1 copy.76
  954.0 5.8 all-to-all-done.2
  (53 shorter events, 12.7 us)
Async XLA Ops:
  7.2 32.2 %copy-start.8 = (bf16[384,512]{1,0:T(8,128)(2,1)S(1)}, bf16[384,512]{1,0:T(8,128)(2,1)}, u32[]{:S(2)}) copy-start(bf16[384,512]{1,0:T(8,128)(2,1)} %param.6) | copy-start | bytes 1179652
  9.7 21.6 %all-to-all-start.1 = ((bf16[8,2,256]{2,1,0:T(2,128)(2,1)}), bf16[8,2,256]{2,1,0:T(2,128)(2,1)S(1)}, u32[]{:S(2)}, u32[]{:S(2)}) async-start(bf16[8,2,256]{2,1,0:T(2,128)(2,1)} %reshape.178), calls=%async_computation.1 | async-start | bytes 16384 | tf_op jit(solution)/shard_map/all_to_all | solution.py:67
  31.3 13.7 %all-to-all-start = ((bf16[8,2,256]{2,1,0:T(2,128)(2,1)}), bf16[8,2,256]{2,1,0:T(2,128)(2,1)S(1)}, u32[]{:S(2)}, u32[]{:S(2)}) async-start(bf16[8,2,256]{2,1,0:T(2,128)(2,1)} %reshape.180), calls=%async_computation | async-start | bytes 16384 | tf_op jit(solution)/shard_map/all_to_all | solution.py:66
  36.0 894.2 %reduce-scatter.4.cloned.1.call-start = ((), (), s32[]{:S(2)}) async-start(), calls=%async_computation.5 | async-start | bytes 2129920
  36.9 316.5 %copy-start = (pred[384,512]{1,0:T(8,128)(4,1)}, pred[384,512]{1,0:T(8,128)(4,1)S(1)}, u32[]{:S(2)}) copy-start(pred[384,512]{1,0:T(8,128)(4,1)S(1)} %broadcast_compare_fusion) | copy-start | bytes 589828
  39.6 312.7 %copy-start.4 = (bf16[384,512]{0,1:T(8,128)(2,1)}, bf16[384,512]{0,1:T(8,128)(2,1)S(1)}, u32[]{:S(2)}) copy-start(bf16[384,512]{0,1:T(8,128)(2,1)S(1)} %copy.88) | copy-start | bytes 1179652
  352.8 1.0 copy-start.6
  358.8 1.8 copy-start.1
  358.8 1.8 copy-start.2
  358.9 1.8 copy-start.7
  360.7 1.0 copy-start.5
  931.2 20.0 %copy-start.3 = (bf16[2,384,256]{1,2,0:T(8,128)(2,1)S(1)}, bf16[2,384,256]{1,2,0:T(8,128)(2,1)}, u32[]{:S(2)}) copy-start(bf16[2,384,256]{1,2,0:T(8,128)(2,1)} %convolution_convert_fusion) | copy-start | bytes 1179652
  932.6 13.5 %all-to-all-start.3 = ((bf16[8,2,256]{2,1,0:T(2,128)(2,1)}), bf16[8,2,256]{2,1,0:T(2,128)(2,1)S(1)}, u32[]{:S(2)}, u32[]{:S(2)}) async-start(bf16[8,2,256]{2,1,0:T(2,128)(2,1)} %reshape.184), calls=%async_computation.3 | async-start | bytes 16384 | tf_op jit(solution)/shard_map/all_to_all | solution.py:146
  946.1 13.7 %all-to-all-start.2 = ((bf16[8,2,256]{2,1,0:T(2,128)(2,1)}), bf16[8,2,256]{2,1,0:T(2,128)(2,1)S(1)}, u32[]{:S(2)}, u32[]{:S(2)}) async-start(bf16[8,2,256]{2,1,0:T(2,128)(2,1)} %reshape.182), calls=%async_computation.2 | async-start | bytes 16384 | tf_op jit(solution)/shard_map/all_to_all | solution.py:143
Sparse Core Ops, SparseCore 0:
  364.3 565.8 reduce-scatter.3
where the time goes:
time: 968 us; the launch traced here: 967 us
  waiting for transfers between devices  591 us (61%)
  blocking collectives  306 us (32%)
  starting transfers between devices  26.5 us (3%)
  local copies, waits for them, and re-layouts  16.2 us (2%)
  between operations  14.3 us (1%)
    unnamed x2, waiting for transfers between devices  566 us
    all_gather x1, blocking collectives, body(): lax.all_gather(key_part, 'seq', axis=0, tiled=True)  158 us
    all_gather x1, blocking collectives, body(): lax.all_gather(value_part, 'seq', axis=0, tiled=True)  148 us
  transfers between devices with their start and end apart: 5, of which 5 were waited for; matrix products, arithmetic and copies ran while one was open for 1% of the time, Pallas kernels for 0%

commit v1 on v0

v1 whole, which is shorter than its diff:
```python
import jax
import jax.numpy as jnp
from jax import lax
from jax.experimental import pallas as pl
from jax.experimental.pallas import tpu as pltpu
from jax.sharding import Mesh, PartitionSpec as P

HD = 256
NEGATIVE = -1e30
NT = (((1,), (1,)), ((), ()))
NN = (((1,), (0,)), ((), ()))
TN = (((0,), (0,)), ((), ()))


def dot(a, b, dims):
    return lax.dot_general(a, b, dims, preferred_element_type=jnp.float32)


def attention_kernel(
    q_ref, g_ref, own_ref, other_ref, ed_ref, dd_ref, ctx_ref, dq_ref, down_ref, dother_ref
):
    half, wide = own_ref.shape
    cols = wide // 2
    scale = HD**-0.5
    allowed = dd_ref[...] == ed_ref[...]
    for head in range(cols // HD):
        at = slice(head * HD, (head + 1) * HD)
        at_v = slice(cols + head * HD, cols + (head + 1) * HD)
        q, g = q_ref[:, at], g_ref[:, at]
        k = jnp.concatenate([own_ref[:, at], other_ref[:, at]], axis=0)
        v = jnp.concatenate([own_ref[:, at_v], other_ref[:, at_v]], axis=0)
        logits = jnp.where(allowed, dot(q, k, NT) * scale, NEGATIVE)
        top = jnp.max(logits, axis=1, keepdims=True)
        terms = jnp.exp(logits - top)
        prob = terms * (1.0 / jnp.sum(terms, axis=1, keepdims=True))
        weights = prob.astype(jnp.bfloat16)
        ctx = dot(weights, v, NN).astype(jnp.bfloat16)
        ctx_ref[:, at] = ctx
        delta = jnp.sum(
            g.astype(jnp.float32) * ctx.astype(jnp.float32), axis=1, keepdims=True
        )
        ds = (prob * (dot(g, v, NT) - delta)).astype(jnp.bfloat16)
        dq_ref[:, at] = dot(ds, k, NN) * scale
        dk = dot(ds, q, TN) * scale
        dv = dot(weights, g, TN)
        down_ref[:, at] = dk[:half]
        down_ref[:, at_v] = dv[:half]
        dother_ref[:, at] = dk[half:].astype(jnp.bfloat16)
        dother_ref[:, at_v] = dv[half:].astype(jnp.bfloat16)


def attention(q, g, own, other, ed, dd):
    rows, cols = q.shape
    return pl.pallas_call(
        attention_kernel,
        out_shape=[
            jax.ShapeDtypeStruct((rows, cols), jnp.bfloat16),
            jax.ShapeDtypeStruct((rows, cols), jnp.float32),
            jax.ShapeDtypeStruct(own.shape, jnp.float32),
            jax.ShapeDtypeStruct(own.shape, jnp.bfloat16),
        ],
        compiler_params=pltpu.CompilerParams(vmem_limit_bytes=48 * 1024 * 1024),
        cost_estimate=pl.CostEstimate(
            flops=24 * rows * own.size // 2,
            bytes_accessed=6 * 1024 * 1024,
            transcendentals=rows * own.shape[0] * 2 * cols // HD,
        ),
    )(q, g, own, other, ed, dd)


def body(queries, enc_keys, enc_values, out_grad, enc_doc, dec_doc):
    size = {a: lax.axis_size(a) for a in "shxyc"}
    rows, cols = queries.shape
    sections, column = size["s"] * size["h"], size["x"] * size["y"]
    pair = [(0, 1), (1, 0)]
    parts = jnp.concatenate(
        [enc_keys.reshape(size["s"], -1, 128), enc_values.reshape(size["s"], -1, 128)], axis=1
    )
    parts = jnp.broadcast_to(parts[None], (size["h"],) + parts.shape)
    parts = parts.reshape((sections,) + parts.shape[2:])
    mine = lax.all_to_all(parts, ("h", "s"), split_axis=0, concat_axis=0, tiled=True)
    mine = mine.reshape(sections, 2 * cols)
    spread = jnp.broadcast_to(mine[None], (column,) + mine.shape)
    own = lax.all_to_all(spread, ("x", "y"), split_axis=0, concat_axis=0, tiled=True)
    own = own.reshape(column * sections, 2 * cols)
    other = lax.ppermute(own, "c", pair)
    docs = enc_doc.reshape([size[a] for a in "shxyc"]).transpose(4, 2, 3, 1, 0)
    docs = docs.reshape(2, -1)
    docs = jnp.where(lax.axis_index("c") == 0, docs, docs[::-1]).reshape(1, -1)
    context, query_grad, grad_own, grad_other = attention(
        queries, out_grad, own, other, docs, dec_doc.reshape(-1, 1)
    )
    came = lax.ppermute(grad_other, "c", pair)
    chip = (grad_own + came.astype(jnp.float32)).astype(jnp.bfloat16)
    chip = chip.reshape(column, sections, 2 * cols)
    plane = lax.all_to_all(chip, ("x", "y"), split_axis=0, concat_axis=0, tiled=True)
    plane = jnp.sum(plane.astype(jnp.float32), axis=0).astype(jnp.bfloat16)
    plane = plane.reshape(sections, -1, 128)
    last = lax.all_to_all(plane, ("h", "s"), split_axis=0, concat_axis=0, tiled=True)
    last = last.reshape((size["h"], size["s"]) + last.shape[1:]).astype(jnp.float32)
    last = jnp.sum(last, axis=0)
    blocks = cols // 128
    key_grad = last[:, :blocks].reshape(1, -1)
    value_grad = last[:, blocks:].reshape(1, -1)
    return context, query_grad, key_grad, value_grad


def solution(mesh):
    inner = Mesh(mesh.devices.reshape(8, 2, 4, 4, 2), ("s", "h", "x", "y", "c"))
    seq = ("h", "x", "y", "c")
    wide, owner = P(seq, "s"), P(("s",) + seq, None)
    return jax.shard_map(
        body,
        mesh=inner,
        in_specs=(wide, owner, owner, wide, P(), P(seq)),
        out_specs=(wide, wide, owner, owner),
        check_vma=False,
    )
```

time: 968 us -> 87.9 us (0.09)
  the two profiles are of different devices: /device:TPU:32 before, /device:TPU:8 now
where the time goes in v1:
time: 87.9 us; the launch traced here: 87.5 us
  blocking collectives  73.8 us (84%)
  starting transfers between devices  4.07 us (5%)
  Pallas kernels  3.45 us (4%)
  waiting for transfers between devices  2.77 us (3%)
  local copies, waits for them, and re-layouts  1.5 us (2%)
  other arithmetic  1.09 us (1%)
    all_to_all x1, blocking collectives, body(): lax.all_to_all(parts, ('h', 's'), split_axis=0, concat_axis=0, tiled=True)  27.6 us
    all_to_all x1, blocking collectives, body(): lax.all_to_all(spread, ('x', 'y'), split_axis=0, concat_axis=0, tiled=True)  16.1 us
    all_to_all x1, blocking collectives, body(): lax.all_to_all(plane, ('h', 's'), split_axis=0, concat_axis=0, tiled=True)  15.2 us
    all_to_all x1, blocking collectives, body(): lax.all_to_all(chip, ('x', 'y'), split_axis=0, concat_axis=0, tiled=True)  15 us
    pallas_call x1, Pallas kernels, attention(): pl.pallas_call(attention_kernel, out_shape=[jax.ShapeDtypeStruct((rows, c...  3.45 us
    ppermute x1, starting transfers between devices, body(): other = lax.ppermute(own, 'c', pair)  2.04 us
    ppermute x1, starting transfers between devices, body(): came = lax.ppermute(grad_other, 'c', pair)  2.03 us
  transfers between devices with their start and end apart: 2, of which 2 were waited for; matrix products, arithmetic and copies ran while one was open for 1% of the time, Pallas kernels for 0%

profile of v1, /device:TPU:8, one launch (start us, length us, event | category | flops | bytes accessed | tf_op | source)
XLA Modules:
  0.0 87.5 jit_solution(13522931443598574569)
XLA Ops:
  0.6 0.8 reduce.1
  1.4 0.1 reduce.2
  1.5 27.6 %all_to_all.20 = bf16[16,8,128]{2,1,0:T(8,128)(2,1)S(1)} all-to-all(bf16[16,8,128]{2,1,0:T(8,128)(2,1)S(1)} %bitcast.27), channel_id=1, replica_groups=mesh['s'=8,'h'=2,'x'=4,'y'=4,'c'=2] {'h','s'}, dimensions={0} | all-to-all | bytes 65536 | tf_op jit(solution)/shard_map/all_to_all | solution.py:81
  29.1 0.1 broadcast_in_dim.15
  29.1 0.0 copy-start.3
  29.1 0.0 copy-start.4
  29.2 0.0 copy-start.1
  29.2 16.1 %all_to_all.21 = bf16[16,16,1024]{2,1,0:T(8,128)(2,1)S(1)} all-to-all(bf16[16,16,1024]{2,1,0:T(8,128)(2,1)S(1)} %broadcast_in_dim.15), channel_id=1, replica_groups=mesh['s'=8,'h'=2,'x'=4,'y'=4,'c'=2] {'x','y'}, dimensions={0} | all-to-all | bytes 1048576 | tf_op jit(solution)/shard_map/all_to_all | solution.py:84
  45.3 2.0 %collective-permute-start = (bf16[256,1024]{1,0:T(8,128)(2,1)S(1)}, bf16[256,1024]{1,0:T(8,128)(2,1)S(1)}, u32[]{:S(2)}, u32[]{:S(2)}) collective-permute-start(bf16[256,1024]{1,0:T(8,128)(2,1)S(1)} %bitcast.20), channel_id=1, source_target_pairs={{0,1},{1,0},{2,3},{3,2},{4,5},{5,4},{6,7},{7,6},{8,9},{9,8},{10,11... | collective-permute-start | bytes 1572872 | tf_op jit(solution)/shard_map/ppermute | solution.py:86
  47.3 0.2 reshape.53
  47.5 0.3 copy.13
  47.8 0.1 reshape.54
  47.9 0.1 rev.3
  48.0 0.1 reshape.62.dd_ref
  48.2 1.0 %collective-permute-done.other_ref = bf16[256,1024]{1,0:T(8,128)(2,1)S(1)} collective-permute-done((bf16[256,1024]{1,0:T(8,128)(2,1)S(1)}, bf16[256,1024]{1,0:T(8,128)(2,1)S(1)}, u32[]{:S(2)}, u32[]{:S(2)}) %collective-permute-start) | collective-permute-done | bytes 524320 | tf_op jit(solution)/shard_map/ppermute | solution.py:86
  49.2 0.0 copy-done.1
  49.2 3.4 %shard_map.93 = (bf16[384,512]{1,0:T(8,128)(2,1)}, f32[384,512]{1,0:T(8,128)}, f32[256,1024]{1,0:T(8,128)S(1)}, bf16[256,1024]{1,0:T(8,128)(2,1)S(1)}) custom-call(bf16[384,512]{1,0:T(8,128)(2,1)S(1)} %copy-done, bf16[384,512]{1,0:T(8,128)(2,1)S(1)} %copy-done.1, bf16[256,1024]{1,0:T(8,128)(2,1)S(1)} %bitcast.21, ...), custom_call_target="tpu_custom_call" | custom-call | flops 1207959552 | bytes 6291456 | tf_op jit(solution)/shard_map/pallas_call | solution.py:54
  52.6 2.0 %collective-permute-start.1 = (bf16[256,1024]{1,0:T(8,128)(2,1)S(1)}, bf16[256,1024]{1,0:T(8,128)(2,1)S(1)}, u32[]{:S(2)}, u32[]{:S(2)}) collective-permute-start(bf16[256,1024]{1,0:T(8,128)(2,1)S(1)} %get-tuple-element.11), channel_id=1, source_target_pairs={{0,1},{1,0},{2,3},{3,2},{4,5},{5,4},{6,7},{7,6},{8,9},{9,8},{10,11... | collective-permute-start | bytes 1572872 | tf_op jit(solution)/shard_map/ppermute | solution.py:93
  54.7 1.8 %collective-permute-done.1 = bf16[256,1024]{1,0:T(8,128)(2,1)S(1)} collective-permute-done((bf16[256,1024]{1,0:T(8,128)(2,1)S(1)}, bf16[256,1024]{1,0:T(8,128)(2,1)S(1)}, u32[]{:S(2)}, u32[]{:S(2)}) %collective-permute-start.1) | collective-permute-done | bytes 524320 | tf_op jit(solution)/shard_map/ppermute | solution.py:93
  56.4 0.2 add_convert_fusion
  56.6 15.0 %all_to_all.22 = bf16[16,16,1024]{2,1,0:T(8,128)(2,1)S(1)} all-to-all(bf16[16,16,1024]{2,1,0:T(8,128)(2,1)S(1)} %bitcast.23), channel_id=1, replica_groups=mesh['s'=8,'h'=2,'x'=4,'y'=4,'c'=2] {'x','y'}, dimensions={0} | all-to-all | bytes 1048576 | tf_op jit(solution)/shard_map/all_to_all | solution.py:96
  71.6 0.1 reduce_sum.21
  71.7 15.2 %all_to_all.23 = bf16[16,8,128]{2,1,0:T(8,128)(2,1)S(1)} all-to-all(bf16[16,8,128]{2,1,0:T(8,128)(2,1)S(1)} %bitcast.29), channel_id=1, replica_groups=mesh['s'=8,'h'=2,'x'=4,'y'=4,'c'=2] {'h','s'}, dimensions={0} | all-to-all | bytes 65536 | tf_op jit(solution)/shard_map/all_to_all | solution.py:99
  86.9 0.6 fusion
  (13 shorter events, 0.1 us)
Async XLA Ops:
  0.6 0.8 copy-start.2
  29.1 18.2 %copy-start.3 = (s32[512]{0:T(512)S(1)}, s32[512]{0:T(512)}, u32[]{:S(2)}) copy-start(s32[512]{0:T(512)} %param.10) | copy-start | bytes 6148
  29.1 18.9 %copy-start.4 = (s32[384]{0:T(512)S(1)}, s32[384]{0:T(512)}, u32[]{:S(2)}) copy-start(s32[384]{0:T(512)} %param.11) | copy-start | bytes 4612
  29.2 20.0 %copy-start.1 = (bf16[384,512]{1,0:T(8,128)(2,1)S(1)}, bf16[384,512]{1,0:T(8,128)(2,1)}, u32[]{:S(2)}) copy-start(bf16[384,512]{1,0:T(8,128)(2,1)} %g_ref.1) | copy-start | bytes 1179652
  45.2 3.9 %copy-start = (bf16[384,512]{1,0:T(8,128)(2,1)S(1)}, bf16[384,512]{1,0:T(8,128)(2,1)}, u32[]{:S(2)}) copy-start(bf16[384,512]{1,0:T(8,128)(2,1)} %q_ref.1) | copy-start | bytes 1179652
  45.3 3.9 %collective-permute-start = (bf16[256,1024]{1,0:T(8,128)(2,1)S(1)}, bf16[256,1024]{1,0:T(8,128)(2,1)S(1)}, u32[]{:S(2)}, u32[]{:S(2)}) collective-permute-start(bf16[256,1024]{1,0:T(8,128)(2,1)S(1)} %bitcast.20), channel_id=1, source_target_pairs={{0,1},{1,0},{2,3},{3,2},{4,5},{5,4},{6,7},{7,6},{8,9},{9,8},{10,11... | collective-permute-start | bytes 1572872 | tf_op jit(solution)/shard_map/ppermute | solution.py:86
  52.6 3.8 %collective-permute-start.1 = (bf16[256,1024]{1,0:T(8,128)(2,1)S(1)}, bf16[256,1024]{1,0:T(8,128)(2,1)S(1)}, u32[]{:S(2)}, u32[]{:S(2)}) collective-permute-start(bf16[256,1024]{1,0:T(8,128)(2,1)S(1)} %get-tuple-element.11), channel_id=1, source_target_pairs={{0,1},{1,0},{2,3},{3,2},{4,5},{5,4},{6,7},{7,6},{8,9},{9,8},{10,11... | collective-permute-start | bytes 1572872 | tf_op jit(solution)/shard_map/ppermute | solution.py:93
